TPU v7x, 32 devices: a whole 2x2x4 slice. The times are simulated.
32 devices in a mesh: chan: 16 (over z, y, core), tm: 2 (over x).
Axes of the slice: x: 2, y: 2, z: 4, core: 2. Of those that a mesh axis runs over, the one named last changes fastest.
Arguments:
- traces: bfloat16 [16, 48, 128, 1024], P('chan', 'tm'), may hold values from -6 to 6
- valid_mask: int32 [16, 48, 1024], P('chan', 'tm'), may hold values 0 or 1
- pair_owner: int32 [16, 4], P('chan'), may hold values from -1 to 15, as said below
Outputs:
- correlations: float32 [16, 4, 101, 128], P('chan')
Inputs may be any that keep to these rules, and one draw needn't show every extreme that they name: `pair_owner`: row r lists distinct owners in r + 1 .. r + 4 (within the cable) in its leading slots, then -1; every reader with a block above it has one pair or more, and reader 0 fills all 4 slots.
All inputs are finite; a program needn't handle non-finite values. No bound on the sum of `valid_mask` on one device may be relied on, other than what follows from the above.
Results may differ from a plain program's by a relative error of at most 0.0052.
Values may be sent and summed in bfloat16 or wider, within the bound.
A program may use at most 64 MiB of HBM per device.

v0:
```python
import math

import jax
import jax.numpy as jnp
from jax import lax
from jax.sharding import PartitionSpec as P

NF = 256
MAXLAG = 50
SMOOTH = 4
REACH = 4


water_level = 0.05
eps = 1e-06


def forward_table(samples_count, bins_count):
    samples = jnp.arange(samples_count, dtype=jnp.int32)
    bins = jnp.arange(1, bins_count + 1, dtype=jnp.int32)
    phase = samples[:, None] * bins[None, :] % samples_count
    angle = phase.astype(jnp.float32) * jnp.float32(2.0 * math.pi / samples_count)
    return jnp.concatenate([jnp.cos(angle), -jnp.sin(angle)], axis=1).astype(jnp.bfloat16)


def inverse_table(samples_count, bins_count, windows_all):
    bins = jnp.arange(1, bins_count + 1, dtype=jnp.int32)
    offsets = jnp.arange(2 * MAXLAG + 1, dtype=jnp.int32) - MAXLAG
    phase = bins[:, None] * offsets[None, :] % samples_count
    angle = phase.astype(jnp.float32) * jnp.float32(2.0 * math.pi / samples_count)
    factor = jnp.float32(1.0 / math.sqrt(windows_all * bins_count))
    return jnp.concatenate([jnp.cos(angle), -jnp.sin(angle)], axis=0) * factor


def whiten(block_traces, block_mask, forward, bins_count):
    masked = block_traces * block_mask[:, None, :].astype(jnp.bfloat16)
    wins, chans, samples = masked.shape
    spectra = jnp.dot(
        masked.reshape(wins * chans, samples), forward, preferred_element_type=jnp.float32
    )
    spectra = spectra.reshape(wins, chans, 2 * bins_count)
    real_part = spectra[..., :bins_count]
    imag_part = spectra[..., bins_count:]
    amplitude = jnp.sqrt(real_part * real_part + imag_part * imag_part)
    padded = jnp.pad(amplitude, ((0, 0), (0, 0), (SMOOTH, SMOOTH)))
    smooth = padded[..., 0:bins_count]
    for j in range(1, 2 * SMOOTH + 1):
        smooth = smooth + padded[..., j : j + bins_count]
    smooth = smooth / jnp.float32(2 * SMOOTH + 1)
    divisor = smooth + water_level * jnp.mean(amplitude, axis=-1, keepdims=True) + eps
    return (spectra / jnp.concatenate([divisor, divisor], axis=-1)).astype(jnp.bfloat16)


def pair_products(left, right):
    return jnp.einsum("nbwc,nbwc->nbc", left, right, preferred_element_type=jnp.float32)


def body(traces, valid_mask, pair_owner):
    wins_here = traces.shape[1]
    samples_count = traces.shape[3]
    bins_count = NF
    windows_all = wins_here * lax.axis_size("tm")
    forward = forward_table(samples_count, bins_count)
    inverse = inverse_table(samples_count, bins_count, windows_all)
    own_spec = whiten(traces[0], valid_mask[0], forward, bins_count)
    reader = lax.axis_index("chan")
    owners = pair_owner[0]
    chans = own_spec.shape[1]
    groups = lax.axis_size("chan")
    layout = own_spec.reshape(wins_here, chans, 2, bins_count).transpose(2, 3, 0, 1)[None]
    blocks = lax.all_to_all(layout, "chan", split_axis=2, concat_axis=0, tiled=True)
    filler = jnp.zeros((REACH,) + blocks.shape[1:], blocks.dtype)
    extended = jnp.concatenate([blocks, filler], axis=0)
    left_real = blocks[:, 0]
    left_imag = blocks[:, 1]
    pieces = []
    for distance in range(1, REACH + 1):
        other = extended[distance : distance + groups]
        right_real = other[:, 0]
        right_imag = other[:, 1]
        real_sum = pair_products(left_real, right_real) + pair_products(left_imag, right_imag)
        imag_sum = pair_products(left_real, right_imag) - pair_products(left_imag, right_real)
        pieces.append(jnp.stack([real_sum, imag_sum], axis=1))
    local_stacks = jnp.stack(pieces, axis=1)
    returned = lax.all_to_all(local_stacks, "chan", split_axis=0, concat_axis=3, tiled=True)
    by_distance = returned[0].reshape(REACH, 2 * bins_count, chans).transpose(0, 2, 1)
    distances = jnp.arange(1, REACH + 1, dtype=jnp.int32)
    chosen = (owners[:, None] == reader + distances[None, :]).astype(jnp.float32)
    stacks = jnp.einsum("pd,dck->pck", chosen, by_distance, precision=lax.Precision.HIGHEST)
    summed = lax.psum(stacks, "tm")
    result = jnp.einsum("pck,kl->plc", summed, inverse, precision=lax.Precision.HIGHEST)
    return result[None]


def solution(mesh):
    return jax.shard_map(
        body,
        mesh=mesh,
        in_specs=(P("chan", "tm", None, None), P("chan", "tm", None), P("chan", None)),
        out_specs=P("chan", None, None, None),
        check_vma=False,
    )
```

profile of v0, /device:TPU:0, one launch (start us, length us, event | category | flops | bytes accessed | tf_op | source)
XLA Modules:
  0.0 217.8 jit_solution(14518581184413098751)
XLA Ops:
  6.5 4.4 %cosine_convert_fusion = (bf16[1024,256]{1,0:T(8,128)(2,1)S(1)}, bf16[1024,256]{1,0:T(8,128)(2,1)S(1)}) fusion(s32[256]{0:T(256)S(1)} %iota_add_fusion), kind=kLoop, calls=%fused_computation.93 | loop fusion | flops 4456448 | bytes 1049600 | tf_op jit(solution)/shard_map/convert
  11.0 0.9 convert_bitcast_fusion
  11.9 5.6 %fusion.1 = f32[24,128,512]{2,1,0:T(8,128)S(1)} fusion(bf16[1,24,128,1024]{3,2,1,0:T(8,128)(2,1)} %param.3, bf16[24,1024]{1,0:T(8,128)(2,1)S(1)} %convert_bitcast_fusion, bf16[1024,256]{1,0:T(8,128)(2,1)S(1)} %get-tuple-element.26, bf16[1024,256]{1,0:T(8,128)(2,1)S(1)} %get-tuple-element.25), kind=kOutput, calls=%fused_computation.27 | convolution fusion | flops 3226468352 | bytes 13680640 | tf_op jit(solution)/shard_map/dot_general | solution.py:38
  17.4 1.2 fusion.67
  18.6 8.3 %fusion.12 = f32[24,128,256]{2,1,0:T(8,128)} fusion(f32[24,128,256]{2,1,0:T(8,128)S(1)} %get-tuple-element.22, f32[24,128]{1,0:T(8,128)S(1)} %broadcast_multiply_fusion), kind=kLoop, calls=%fused_computation.46 | loop fusion | flops 8650752 | bytes 6303744 | tf_op jit(solution)/shard_map/add | solution.py:50
  26.9 5.4 %fusion = bf16[24,128,512]{2,1,0:T(8,128)(2,1)} fusion(f32[24,128,512]{2,1,0:T(8,128)S(1)} %fusion.1, f32[24,128,256]{2,1,0:T(8,128)} %fusion.12), kind=kLoop, calls=%fused_computation.25 | loop fusion | flops 4718592 | bytes 12582912 | tf_op jit(solution)/shard_map/convert_element_type | solution.py:51
  32.3 3.8 %reshape.41 = bf16[24,128,2,256]{3,2,1,0:T(2,128)(2,1)S(1)} reshape(bf16[24,128,512]{2,1,0:T(8,128)(2,1)} %fusion) | data formatting | bytes 6291456 | tf_op jit(solution)/shard_map/reshape | solution.py:70
  36.0 5.8 %copy.12 = bf16[24,128,2,256]{1,0,2,3:T(8,128)(2,1)} copy(bf16[24,128,2,256]{3,2,1,0:T(2,128)(2,1)S(1)} %reshape.41) | data formatting | bytes 6291456 | tf_op jit(solution)/shard_map/reshape | solution.py:70
  41.8 77.2 %all_to_all.33 = bf16[1,2,256,24,128]{4,3,1,0,2:T(8,128)(2,1)S(1)} all-to-all(bf16[1,2,256,24,128]{4,3,1,0,2:T(8,128)(2,1)} %bitcast.209), channel_id=1, replica_groups=mesh['chan'=16,'tm'=2] {'chan'}, dimensions={2} | all-to-all | bytes 6291456 | tf_op jit(solution)/shard_map/all_to_all | solution.py:71
  119.0 0.5 copy.13
  119.5 7.2 %fusion.21 = (f32[16,16,128]{2,1,0:T(8,128)S(1)}, f32[16,16,128]{2,1,0:T(8,128)S(1)}, f32[16,16,128]{2,1,0:T(8,128)S(1)}, f32[16,16,128]{2,1,0:T(8,128)S(1)}, f3...) fusion(bf16[16,2,16,24,128]{4,3,2,0,1:T(8,128)(2,1)S(1)} %bitca, ...), kind=kLoop, calls=%fused_computation.55 | loop fusion | flops 22511616 | bytes 7471104 | tf_op jit(solution)/shard_map/nbwc,nbwc->nbc/dot_general | solution.py:55
  126.7 6.1 %fusion.13 = (f32[16,16,128]{2,1,0:T(8,128)S(1)}, f32[16,16,128]{2,1,0:T(8,128)S(1)}, f32[16,16,128]{2,1,0:T(8,128)S(1)}, f32[16,16,128]{2,1,0:T(8,128)S(1)}, f3...) fusion(bf16[16,2,16,24,128]{4,3,2,0,1:T(8,128)(2,1)S(1)} %bitcast.208), kind=kLoop, calls=%fused_computation.47 | loop fusion | flops 17858560 | bytes 7208960 | tf_op jit(solution)/shard_map/nbwc,nbwc->nbc/dot_general | solution.py:55
  133.1 1.1 pad_maximum_fusion
  134.2 0.0 copy-start
  134.2 5.3 %all-to-all-start.1 = ((f32[16,4,2,16,128]{4,3,2,1,0:T(8,128)}), f32[16,4,2,16,128]{4,3,2,1,0:T(8,128)S(1)}, u32[]{:S(2)}, u32[]{:S(2)}) async-start(f32[16,4,2,16,128]{4,3,2,1,0:T(8,128)} %pad_maximum_fusion), calls=%async_computation.1 | async-start | bytes 2097152 | tf_op jit(solution)/shard_map/all_to_all | solution.py:85
  139.5 0.0 all-reduce.4.cloned.1.call-start
  139.6 22.9 %all-to-all-done.1 = f32[16,4,2,16,128]{4,3,2,1,0:T(8,128)S(1)} async-done(((f32[16,4,2,16,128]{4,3,2,1,0:T(8,128)}), f32[16,4,2,16,128]{4,3,2,1,0:T(8,128)S(1)}, u32[]{:S(2)}, u32[]{:S(2)}) %all-to-all-start.1) | async-done | bytes 1048608 | tf_op jit(solution)/shard_map/all_to_all | solution.py:85
  162.4 0.1 copy.14
  162.5 0.5 copy.15
  163.0 0.0 copy-done
  163.1 2.2 fusion.45
  165.2 0.0 all-reduce.4.cloned.1.call-update
  165.3 0.5 fusion.59
  165.8 41.9 %all-reduce.4.cloned.1.call-done = f32[4,128,512]{2,0,1:T(4,128)} async-done(((f32[4,128,512]{2,0,1:T(4,128)}), f32[4,128,512]{2,0,1:T(4,128)}) %all-reduce.4.cloned.1.call-update) | async-done | bytes 1048592 | tf_op jit(solution)/shard_map/psum | solution.py:90
  207.6 2.5 %convolution_bitcast_fusion = f32[1,4,101,128]{3,2,1,0:T(8,128)S(1)} fusion(f32[4,128,512]{2,0,1:T(4,128)} %all-reduce.4.cloned.1.call-done, f32[256,101]{0,1:T(8,128)S(1)} %get-tuple-element.24, f32[256,101]{0,1:T(8,128)S(1)} %get-tuple-element.23), kind=kOutput, calls=%fused_computation.81 | convolution fusion | flops 317821952 | bytes 1462272 | tf_op jit(solution)/shard_map/pck,kl->plc/dot_general | solution.py:91
  210.2 0.7 copy.17
  (12 shorter events, 0.2 us)
Async XLA Ops:
  134.2 28.9 %copy-start = (s32[1,4]{1,0:T(1,128)S(1)}, s32[1,4]{1,0:T(1,128)}, u32[]{:S(2)}) copy-start(s32[1,4]{1,0:T(1,128)} %param.5) | copy-start | bytes 52
  134.2 28.3 %all-to-all-start.1 = ((f32[16,4,2,16,128]{4,3,2,1,0:T(8,128)}), f32[16,4,2,16,128]{4,3,2,1,0:T(8,128)S(1)}, u32[]{:S(2)}, u32[]{:S(2)}) async-start(f32[16,4,2,16,128]{4,3,2,1,0:T(8,128)} %pad_maximum_fusion), calls=%async_computation.1 | async-start | bytes 2097152 | tf_op jit(solution)/shard_map/all_to_all | solution.py:85
  139.5 68.1 %all-reduce.4.cloned.1.call-start = ((), (), s32[]{:S(2)}) async-start(), calls=%async_computation.2 | async-start | bytes 2097152 | tf_op jit(solution)/shard_map/psum | solution.py:90
Sparse Core Ops, SparseCore 0:
  165.4 42.2 all-reduce.3
where the time goes:
time: 218 us
  blocking collectives  77.2 us (35%)
  waiting for transfers between devices  64.8 us (30%)
  other arithmetic  35.2 us (16%)
  between operations  13.6 us (6%)
  local copies, waits for them, and re-layouts  11.4 us (5%)
  matrix products  10.3 us (5%)
  starting transfers between devices  5.36 us (2%)
    all_to_all x1, blocking collectives, body(): lax.all_to_all(layout, 'chan', split_axis=2, concat_axis=0, tiled=True)  77.2 us
    psum x1, waiting for transfers between devices, body(): summed = lax.psum(stacks, 'tm')  41.9 us
    all_to_all x1, waiting for transfers between devices, body(): lax.all_to_all(local_stacks, 'chan', split_axis=0, concat_axis=3, tiled=T...  22.9 us
    dot_general x2, other arithmetic, pair_products(): jnp.einsum('nbwc,nbwc->nbc', left, right, preferred_element_type=jnp.floa...  13.2 us
    reshape x2, local copies, waits for them, and re-layouts, body(): own_spec.reshape(wins_here, chans, 2, bins_count).transpose(2, 3, 0, 1)  9.56 us
    add x1, other arithmetic, whiten(): smooth + water_level * jnp.mean(amplitude, axis=-1, keepdims=True) + eps  8.26 us
    dot_general x1, matrix products, whiten(): jnp.dot(masked.reshape(wins * chans, samples), forward, preferred_element...  5.57 us
    convert_element_type x1, other arithmetic, whiten(): (spectra / jnp.concatenate([divisor, divisor], axis=-1)).astype(jnp.bfloa...  5.35 us
  transfers between devices with their start and end apart: 2, of which 2 were waited for; matrix products, arithmetic and copies ran while one was open for 0% of the time, Pallas kernels for 0%

commit v1 on v0

v1 whole, which is shorter than its diff:
```python
import functools
import math

import jax
import jax.numpy as jnp
import ml_dtypes
import numpy as np
from jax import lax
from jax.experimental import pallas as pl
from jax.experimental.pallas import tpu as pltpu
from jax.sharding import PartitionSpec as P

NF = 256
MAXLAG = 50
LAGS = 2 * MAXLAG + 1
SMOOTH = 4
REACH = 4
LAG_PAD = 128
LAG_ROWS = 104

WATER = 0.05
EPS = 1e-06

MESH = pl.DeviceIdType.MESH

BIG = [
    (0, 1), (0, 2), (0, 3), (0, 4),
    (1, 2), (1, 3), (1, 4), (1, 5),
    (2, 3), (2, 4), (2, 5),
    (3, 4), (3, 5),
    (4, 5),
]
SMALL = [(0, 2), (1, 2), (1, 3)]


def forward_table(samples_count):
    samples = np.arange(samples_count)
    bins = np.arange(1, NF + 1)
    angle = (samples[:, None] * bins[None, :] % samples_count) * (2.0 * math.pi / samples_count)
    return np.concatenate([np.cos(angle), -np.sin(angle)], axis=1).astype(ml_dtypes.bfloat16)


def inverse_table(samples_count, windows_all):
    bins = np.arange(1, NF + 1)
    offsets = np.arange(LAGS) - MAXLAG
    angle = (bins[:, None] * offsets[None, :] % samples_count) * (2.0 * math.pi / samples_count)
    table = np.concatenate([np.cos(angle), -np.sin(angle)], axis=0) / math.sqrt(windows_all * NF)
    return np.pad(table, ((0, 0), (0, LAG_PAD - LAGS))).astype(np.float32)


def smooth_table():
    bins = np.arange(NF)
    band = (np.abs(bins[:, None] - bins[None, :]) <= SMOOTH).astype(np.float32)
    return np.concatenate([band, np.ones((NF, NF), np.float32)], axis=0).astype(ml_dtypes.bfloat16)


def kernel(
    groups, planes,
    traces, mask, forward, smoother, inverse,
    out,
    tbuf, fbuf, maskx, own, big, small, cross_big, cross_small, res_big, res_small, rbuf,
    tsem, fsem, send_sem, big_sem, small_sem, rsend, rsem,
):
    wins = traces.shape[0]
    rows = own.shape[3]
    me = lax.axis_index("chan")
    tm = lax.axis_index("tm")
    core = lax.rem(me, 2)
    y = lax.rem(me // 2, 2)
    z = me // 4
    depth = groups // 4
    has_up = z < depth - 1
    has_down = z > 0
    has_big = jnp.where(y == 0, depth - 1 - z, z) > 0
    has_small = jnp.where(y == 0, z, depth - 1 - z) > 0
    big_base = 4 * z - 2 * y
    small_base = 4 * z - 4 + 6 * y

    def channel_start(p):
        return (p % 2) * 64 + ((p // 2) % 2) * 32 + (p // 4) * 16

    def load(p):
        return pltpu.make_async_copy(
            traces.at[:, pl.ds(pl.multiple_of(channel_start(p), 16), 16), :], tbuf.at[p], tsem.at[p]
        )

    load(0).start()
    table_copy = pltpu.make_async_copy(forward, fbuf, fsem)
    table_copy.start()
    for p in range(1, 8):
        load(p).start()

    barrier = pltpu.get_barrier_semaphore()
    for dz in (-1, 0, 1):
        zz = z + dz

        @pl.when((zz >= 0) & (zz < depth))
        def _():
            for k in range(4):
                for t in range(planes):

                    @pl.when((zz * 4 + k != me) | (t != tm))
                    def _():
                        pl.semaphore_signal(
                            barrier, inc=1, device_id={"chan": zz * 4 + k, "tm": t}, device_id_type=MESH
                        )

    near = 1 + has_up.astype(jnp.int32) + has_down.astype(jnp.int32)
    partners = near * (4 * planes) - 1

    for w in range(wins):
        row = mask[w : w + 1, :].astype(jnp.float32)
        maskx[w] = jnp.broadcast_to(row, (16, row.shape[1])).astype(jnp.bfloat16)

    def chunk_copies(e, c, j, act, act_local):
        src = own.at[e, c, j]
        slot = (e * 2 + c) * 4 + j
        is_big = e == y
        zt = z + 2 * e - 1
        has_z = (zt >= 0) & (zt < depth)

        def remote(dst, kind, recv, chan):
            act(
                pltpu.make_async_remote_copy(
                    src_ref=src, dst_ref=dst, send_sem=send_sem.at[slot, kind], recv_sem=recv,
                    device_id={"chan": chan}, device_id_type=MESH,
                )
            )

        @pl.when(is_big & has_z)
        def _():
            remote(big.at[j, 4 * (1 - y) + core], 0, big_sem.at[j], zt * 4 + y * 2 + c)

        @pl.when(jnp.logical_not(is_big))
        def _():
            remote(big.at[j, 2 + core], 1, big_sem.at[j], z * 4 + (1 - y) * 2 + c)

        @pl.when(jnp.logical_not(is_big) & has_z)
        def _():
            remote(small.at[j, 2 * (1 - e) + core], 0, small_sem.at[j], zt * 4 + y * 2 + c)

        @pl.when(is_big & (c != core))
        def _():
            remote(big.at[j, 4 * y + core], 2, big_sem.at[j], z * 4 + y * 2 + c)

        @pl.when(jnp.logical_not(is_big) & has_small & (c != core))
        def _():
            remote(small.at[j, 2 * (1 - y) + core], 2, small_sem.at[j], z * 4 + y * 2 + c)

        if act_local:

            @pl.when(is_big & (c == core))
            def _():
                pltpu.make_async_copy(src, big.at[j, 4 * y + core], big_sem.at[j]).start()

            @pl.when(jnp.logical_not(is_big) & has_small & (c == core))
            def _():
                pltpu.make_async_copy(src, small.at[j, 2 * (1 - y) + core], small_sem.at[j]).start()

    def start(copy):
        copy.start()

    def wait_send(copy):
        copy.wait_send()

    table_copy.wait()

    def produce(p, carry):
        e = lax.rem(p, 2)
        c = lax.rem(p // 2, 2)
        half = p // 4
        load(p).wait()
        x = (tbuf[p] * maskx[...]).reshape(wins * 16, tbuf.shape[3])
        spectra = jnp.dot(x, fbuf[...], preferred_element_type=jnp.float32)
        real = spectra[:, :NF]
        imag = spectra[:, NF:]
        amplitude = jnp.sqrt(real * real + imag * imag)
        scaled = amplitude * jnp.float32((2 * SMOOTH + 1) * WATER / NF)
        both = jnp.concatenate([amplitude.astype(jnp.bfloat16), scaled.astype(jnp.bfloat16)], axis=1)
        total = jnp.dot(both, smoother[...], preferred_element_type=jnp.float32)
        gain = jnp.float32(2 * SMOOTH + 1) / (total + jnp.float32((2 * SMOOTH + 1) * EPS))
        for part, lo in ((real, 0), (imag, NF)):
            white = (part * gain).reshape(wins, 16, NF)
            for h in range(2):
                own[e, c, 2 * half + h, :, lo : lo + NF] = (
                    white[:, 8 * h : 8 * h + 8, :].reshape(wins * 8, NF).astype(jnp.bfloat16)
                )

        @pl.when(p == 0)
        def _():
            pl.semaphore_wait(barrier, partners)

        chunk_copies(e, c, half, start, True)
        return carry

    lax.fori_loop(0, 8, produce, 0)

    def cross(buf, j, pairs, result):
        used = sorted({s for pair in pairs for s in pair})
        for f in range(NF // 128):
            lo = f * 128

            def step(i, sums):
                r = pl.ds(pl.multiple_of(i * 16, 16), 16)
                re = {s: buf[j, s, r, lo : lo + 128].astype(jnp.float32) for s in used}
                im = {s: buf[j, s, r, NF + lo : NF + lo + 128].astype(jnp.float32) for s in used}
                new = []
                for n, (a, b) in enumerate(pairs):
                    direct = re[a] * re[b] + im[a] * im[b]
                    crossed = re[a] * im[b] - im[a] * re[b]
                    new.append(sums[2 * n] + (direct[:8] + direct[8:]))
                    new.append(sums[2 * n + 1] + (crossed[:8] + crossed[8:]))
                return tuple(new)

            zero = jnp.zeros((8, 128), jnp.float32)
            sums = lax.fori_loop(0, rows // 16, step, (zero,) * (2 * len(pairs)))
            for n in range(len(pairs)):
                result[8 * n : 8 * n + 8, lo : lo + 128] = sums[2 * n]
                result[8 * n : 8 * n + 8, NF + lo : NF + lo + 128] = sums[2 * n + 1]

    def lags(result):
        return jnp.dot(
            result[...], inverse[...], precision=lax.Precision.HIGHEST, preferred_element_type=jnp.float32
        ).reshape(-1, 8, LAG_PAD)

    def messages(res, j, base, e, first, listed, act, act_local):
        at = pl.ds(pl.multiple_of(e * 64 + core * 32 + j * 8, 8), 8)
        for k, (s, pair, count, distance) in enumerate(listed):
            chan = base + s
            src = res.at[j, pl.ds(pair, count)]
            dst = rbuf.at[tm, pl.ds(distance, count), at]
            for t in range(planes):
                mine = (chan == me) & (t == tm)

                @pl.when(jnp.logical_not(mine))
                def _():
                    act(
                        pltpu.make_async_remote_copy(
                            src_ref=src, dst_ref=dst, send_sem=rsend.at[first + k, t], recv_sem=rsem,
                            device_id={"chan": chan, "tm": t}, device_id_type=MESH,
                        )
                    )

                if act_local:

                    @pl.when(mine)
                    def _():
                        pltpu.make_async_copy(src, dst, rsem).start()

    def big_messages(j, act, act_local):
        send = functools.partial(messages, res_big, j, big_base, y, 0)

        @pl.when((y == 0) & has_big)
        def _():
            send([(0, 0, 4, 0), (1, 4, 4, 0), (2, 8, 3, 0), (3, 11, 2, 0)], act, act_local)

        @pl.when((y == 0) & jnp.logical_not(has_big))
        def _():
            send([(0, 0, 3, 0), (1, 4, 2, 0), (2, 8, 1, 0)], act, act_local)

        @pl.when((y == 1) & has_big)
        def _():
            send([(0, 1, 3, 1), (1, 4, 4, 0), (2, 8, 3, 0), (3, 11, 2, 0), (4, 13, 1, 0)], act, act_local)

        @pl.when((y == 1) & jnp.logical_not(has_big))
        def _():
            send([(2, 8, 3, 0), (3, 11, 2, 0), (4, 13, 1, 0)], act, act_local)

    def small_messages(j, act, act_local):
        @pl.when(has_small)
        def _():
            messages(res_small, j, small_base, 1 - y, 5, [(0, 0, 1, 3), (1, 1, 2, 2)], act, act_local)

    def correlate(j, carry):
        @pl.when(has_small)
        def _():
            pltpu.make_async_copy(small.at[j], small.at[j], small_sem.at[j]).wait()

        @pl.when(has_big)
        def _():
            pltpu.make_async_copy(big.at[j], big.at[j], big_sem.at[j]).wait()

        @pl.when(jnp.logical_not(has_big))
        def _():
            there = big.at[j, pl.ds(2 * y, 4)]
            pltpu.make_async_copy(there, there, big_sem.at[j]).wait()

        @pl.when(j < 2)
        def _():
            for c in range(2):
                for e in range(2):
                    chunk_copies(e, c, j + 2, start, True)

        @pl.when(j > 0)
        def _():
            big_messages(j - 1, wait_send, False)
            small_messages(j - 1, wait_send, False)

        cross(big, j, BIG, cross_big)
        res_big[j] = lags(cross_big)
        big_messages(j, start, True)

        @pl.when(has_small)
        def _():
            cross(small, j, SMALL, cross_small)
            res_small[j] = lags(cross_small)

        small_messages(j, start, True)
        return carry

    lax.fori_loop(0, 4, correlate, 0)
    big_messages(3, wait_send, False)
    small_messages(3, wait_send, False)

    def drain(n, carry):
        chunk_copies(n // 8, lax.rem(n // 4, 2), lax.rem(n, 4), wait_send, False)
        return carry

    lax.fori_loop(0, 16, drain, 0)

    valid = jnp.minimum(REACH, groups - 1 - me)
    for n in range(1, REACH + 1):

        @pl.when(valid == n)
        def _():
            whole = rbuf.at[:, pl.ds(0, n)]
            pltpu.make_async_copy(whole, whole, rsem).wait()

    for d in range(REACH):

        @pl.when(d < valid)
        def _():
            total = rbuf[0, d]
            for t in range(1, planes):
                total = total + rbuf[t, d]
            out[d] = total.T[:LAG_ROWS]

        @pl.when(d >= valid)
        def _():
            out[d] = jnp.zeros(out.shape[1:], jnp.float32)


def body(traces, valid_mask, pair_owner):
    _, wins, chans, samples = traces.shape
    groups = lax.axis_size("chan")
    planes = lax.axis_size("tm")
    rows = wins * 8
    vmem = pl.BlockSpec(memory_space=pltpu.VMEM)
    hbm = pl.BlockSpec(memory_space=pl.ANY)
    f32, bf16 = jnp.float32, jnp.bfloat16
    sums = pl.pallas_call(
        functools.partial(kernel, groups, planes),
        out_shape=jax.ShapeDtypeStruct((REACH, LAG_ROWS, chans), f32),
        in_specs=[hbm, vmem, hbm, vmem, vmem],
        out_specs=vmem,
        scratch_shapes=[
            pltpu.VMEM((8, wins, 16, samples), bf16),
            pltpu.VMEM((samples, 2 * NF), bf16),
            pltpu.VMEM((wins, 16, samples), bf16),
            pltpu.VMEM((2, 2, 4, rows, 2 * NF), bf16),
            pltpu.VMEM((4, 6, rows, 2 * NF), bf16),
            pltpu.VMEM((4, 4, rows, 2 * NF), bf16),
            pltpu.VMEM((len(BIG) * 8, 2 * NF), f32),
            pltpu.VMEM((len(SMALL) * 8, 2 * NF), f32),
            pltpu.VMEM((4, len(BIG), 8, LAG_PAD), f32),
            pltpu.VMEM((4, len(SMALL), 8, LAG_PAD), f32),
            pltpu.VMEM((planes, REACH, chans, LAG_PAD), f32),
            pltpu.SemaphoreType.DMA((8,)),
            pltpu.SemaphoreType.DMA,
            pltpu.SemaphoreType.DMA((16, 3)),
            pltpu.SemaphoreType.DMA((4,)),
            pltpu.SemaphoreType.DMA((4,)),
            pltpu.SemaphoreType.DMA((7, planes)),
            pltpu.SemaphoreType.DMA,
        ],
        compiler_params=pltpu.CompilerParams(
            collective_id=0, has_side_effects=True, vmem_limit_bytes=56 * 1024 * 1024
        ),
        name="correlate",
    )(
        traces[0],
        valid_mask[0],
        jnp.asarray(forward_table(samples)),
        jnp.asarray(smooth_table()),
        jnp.asarray(inverse_table(samples, wins * planes)),
    )
    reader = lax.axis_index("chan")
    owners = pair_owner[0]
    result = jnp.zeros((REACH, LAGS, chans), f32)
    for d in range(REACH):
        chosen = (owners == reader + d + 1)[:, None, None]
        result = result + jnp.where(chosen, sums[d, :LAGS][None], jnp.float32(0))
    return result[None]


def solution(mesh):
    return jax.shard_map(
        body,
        mesh=mesh,
        in_specs=(P("chan", "tm", None, None), P("chan", "tm", None), P("chan", None)),
        out_specs=P("chan", None, None, None),
        check_vma=False,
    )
```

time: 218 us -> 56.9 us (0.26)
  blocking collectives: 77.2 us -> 0 us
  waiting for transfers between devices: 64.8 us -> 0 us
  Pallas kernels: 0 us -> 54.9 us
  other arithmetic: 35.2 us -> 0.89 us
  between operations: 13.6 us -> 0.03 us
  local copies, waits for them, and re-layouts: 11.4 us -> 0.91 us
  matrix products: 10.3 us -> 0 us
  starting transfers between devices: 5.36 us -> 0 us
    all_to_all x1 -> x0, blocking collectives: 77.2 us -> none  [body(): lax.all_to_all(layout, 'chan', split_axis=2, concat_axis=0, tiled=True)]
    pallas_call x0 -> x1, Pallas kernels: none -> 54.9 us  [body(): pl.pallas_call(functools.partial(kernel, groups, planes), out_shape=jax.S...]
    psum x1 -> x0, waiting for transfers between devices: 41.9 us -> none  [body(): summed = lax.psum(stacks, 'tm')]
    all_to_all x1 -> x0, waiting for transfers between devices: 22.9 us -> none  [body(): lax.all_to_all(local_stacks, 'chan', split_axis=0, concat_axis=3, tiled=T...]
    dot_general x2 -> x0, other arithmetic: 13.2 us -> none  [pair_products(): jnp.einsum('nbwc,nbwc->nbc', left, right, preferred_element_type=jnp.floa...]
    dot_general x3 -> x0, matrix products: 10.3 us -> none  [the longest x1 5.57 us: whiten(): jnp.dot(masked.reshape(wins * chans, samples), forward, preferred_element...]
    reshape x2 -> x0, local copies, waits for them, and re-layouts: 9.56 us -> none  [body(): own_spec.reshape(wins_here, chans, 2, bins_count).transpose(2, 3, 0, 1)]
    add x3 -> x1, other arithmetic: 8.27 us -> 0.88 us  [body(): result = result + jnp.where(chosen, sums[d, :LAGS][None], jnp.float32(0))]
  transfers between devices with their start and end apart: 2 -> 0, of which waited for: 2 -> 0; matrix products, arithmetic and copies ran while one was open for 0% -> 0% of each run, Pallas kernels for 0% -> 0%
where the time goes in v1:
time: 56.9 us; the launch traced here: 56.7 us
  Pallas kernels  54.9 us (96%)
  local copies, waits for them, and re-layouts  0.91 us (2%)
  other arithmetic  0.89 us (2%)
    pallas_call x1, Pallas kernels, body(): pl.pallas_call(functools.partial(kernel, groups, planes), out_shape=jax.S...  54.9 us

profile of v1, /device:TPU:0, one launch (start us, length us, event | category | flops | bytes accessed | tf_op | source)
XLA Modules:
  0.0 56.7 jit_solution(17408116273616044883)
XLA Ops:
  0.0 0.0 copy-start
  0.0 54.9 %correlate.1 = f32[4,104,128]{2,1,0:T(8,128)} custom-call(bf16[24,128,1024]{2,1,0:T(8,128)(2,1)} %bitcast.18, s32[24,1024]{1,0:T(8,128)} %bitcast.19, bf16[1024,512]{1,0:T(8,128)(2,1)} %constant.24.clone.forward, bf16[512,256]{1,0:T(8,128)(2,1)} %constant.25.clone.smoother, f32[512,128]{1,0:T(8,128)} %constant.26.clone.inverse), custom_call_target="tpu_custom_call" | custom-call | tf_op jit(solution)/shard_map/correlate/pallas_call | solution.py:351
  54.9 0.9 %slice_bitcast_fusion.3 = (f32[101,128]{1,0:T(8,128)S(1)}, f32[101,128]{1,0:T(8,128)S(1)}, f32[101,128]{1,0:T(8,128)S(1)}, f32[101,128]{1,0:T(8,128)S(1)}) fusion(f32[4,104,128]{2,1,0:T(8,128)} %correlate.1), kind=kLoop, calls=%fused_computation.4 | loop fusion | bytes 413696 | tf_op jit(solution)/shard_map/jit(_where)/broadcast_in_dim | solution.py:392
  55.8 0.0 copy-done
  55.9 0.9 %select_add_fusion = f32[1,4,101,128]{3,1,2,0:T(4,128)} fusion(f32[101,128]{1,0:T(8,128)S(1)} %get-tuple-element.6, f32[101,128]{1,0:T(8,128)S(1)} %get-tuple-element.7, f32[101,128]{1,0:T(8,128)S(1)} %get-tuple-element.8, f32[101,128]{1,0:T(8,128)S(1)} %get-tuple-element.5, pred[4]{0:T(512)(128)(4,1)S(1)} %get-tuple-element.11, ...), kind=kLoop, calls=%fused_computation | loop fusion | flops 361984 | bytes 413712 | tf_op jit(solution)/shard_map/add | solution.py:392
  (1 shorter events, 0.0 us)
Async XLA Ops:
  0.0 55.8 %copy-start = (s32[1,4]{1,0:T(1,128)S(1)}, s32[1,4]{1,0:T(1,128)}, u32[]{:S(2)}) copy-start(s32[1,4]{1,0:T(1,128)} %param.8) | copy-start | bytes 52

commit v2 on v1

--- a/solution.py
+++ b/solution.py
@@ -16,7 +16,6 @@
 SMOOTH = 4
 REACH = 4
 LAG_PAD = 128
-LAG_ROWS = 104
 
 WATER = 0.05
 EPS = 1e-06
@@ -45,7 +44,10 @@
     offsets = np.arange(LAGS) - MAXLAG
     angle = (bins[:, None] * offsets[None, :] % samples_count) * (2.0 * math.pi / samples_count)
     table = np.concatenate([np.cos(angle), -np.sin(angle)], axis=0) / math.sqrt(windows_all * NF)
-    return np.pad(table, ((0, 0), (0, LAG_PAD - LAGS))).astype(np.float32)
+    table = np.pad(table, ((0, 0), (0, LAG_PAD - LAGS))).astype(np.float32)
+    high = table.astype(ml_dtypes.bfloat16)
+    low = (table - high.astype(np.float32)).astype(ml_dtypes.bfloat16)
+    return np.concatenate([high, high, low], axis=0)
 
 
 def smooth_table():
@@ -58,7 +60,7 @@
     groups, planes,
     traces, mask, forward, smoother, inverse,
     out,
-    tbuf, fbuf, maskx, own, big, small, cross_big, cross_small, res_big, res_small, rbuf,
+    tbuf, fbuf, maskx, own, big, small, cross_sum, res, rbuf,
     tsem, fsem, send_sem, big_sem, small_sem, rsend, rsem,
 ):
     wins = traces.shape[0]
@@ -195,7 +197,13 @@
 
     lax.fori_loop(0, 8, produce, 0)
 
-    def cross(buf, j, pairs, result):
+    def send_rest(n, carry):
+        chunk_copies(lax.rem(n, 2), lax.rem(n // 2, 2), 2 + n // 4, start, True)
+        return carry
+
+    lax.fori_loop(0, 8, send_rest, 0)
+
+    def cross(buf, j, pairs, first):
         used = sorted({s for pair in pairs for s in pair})
         for f in range(NF // 128):
             lo = f * 128
@@ -215,15 +223,18 @@
             zero = jnp.zeros((8, 128), jnp.float32)
             sums = lax.fori_loop(0, rows // 16, step, (zero,) * (2 * len(pairs)))
             for n in range(len(pairs)):
-                result[8 * n : 8 * n + 8, lo : lo + 128] = sums[2 * n]
-                result[8 * n : 8 * n + 8, NF + lo : NF + lo + 128] = sums[2 * n + 1]
-
-    def lags(result):
+                cross_sum[first + 8 * n : first + 8 * n + 8, lo : lo + 128] = sums[2 * n]
+                cross_sum[first + 8 * n : first + 8 * n + 8, NF + lo : NF + lo + 128] = sums[2 * n + 1]
+
+    def lags():
+        value = cross_sum[...]
+        high = value.astype(jnp.bfloat16)
+        low = (value - high.astype(jnp.float32)).astype(jnp.bfloat16)
         return jnp.dot(
-            result[...], inverse[...], precision=lax.Precision.HIGHEST, preferred_element_type=jnp.float32
+            jnp.concatenate([high, low, high], axis=1), inverse[...], preferred_element_type=jnp.float32
         ).reshape(-1, 8, LAG_PAD)
 
-    def messages(res, j, base, e, first, listed, act, act_local):
+    def messages(j, base, e, first, listed, act, act_local):
         at = pl.ds(pl.multiple_of(e * 64 + core * 32 + j * 8, 8), 8)
         for k, (s, pair, count, distance) in enumerate(listed):
             chan = base + s
@@ -248,7 +259,7 @@
                         pltpu.make_async_copy(src, dst, rsem).start()
 
     def big_messages(j, act, act_local):
-        send = functools.partial(messages, res_big, j, big_base, y, 0)
+        send = functools.partial(messages, j, big_base, y, 0)
 
         @pl.when((y == 0) & has_big)
         def _():
@@ -269,7 +280,7 @@
     def small_messages(j, act, act_local):
         @pl.when(has_small)
         def _():
-            messages(res_small, j, small_base, 1 - y, 5, [(0, 0, 1, 3), (1, 1, 2, 2)], act, act_local)
+            messages(j, small_base, 1 - y, 5, [(0, 14, 1, 3), (1, 15, 2, 2)], act, act_local)
 
     def correlate(j, carry):
         @pl.when(has_small)
@@ -285,26 +296,19 @@
             there = big.at[j, pl.ds(2 * y, 4)]
             pltpu.make_async_copy(there, there, big_sem.at[j]).wait()
 
-        @pl.when(j < 2)
-        def _():
-            for c in range(2):
-                for e in range(2):
-                    chunk_copies(e, c, j + 2, start, True)
-
         @pl.when(j > 0)
         def _():
             big_messages(j - 1, wait_send, False)
             small_messages(j - 1, wait_send, False)
 
-        cross(big, j, BIG, cross_big)
-        res_big[j] = lags(cross_big)
+        cross(big, j, BIG, 0)
+
+        @pl.when(has_small)
+        def _():
+            cross(small, j, SMALL, 8 * len(BIG))
+
+        res[j] = lags()
         big_messages(j, start, True)
-
-        @pl.when(has_small)
-        def _():
-            cross(small, j, SMALL, cross_small)
-            res_small[j] = lags(cross_small)
-
         small_messages(j, start, True)
         return carry
 
@@ -333,7 +337,7 @@
             total = rbuf[0, d]
             for t in range(1, planes):
                 total = total + rbuf[t, d]
-            out[d] = total.T[:LAG_ROWS]
+            out[d] = total.T[:LAGS]
 
         @pl.when(d >= valid)
         def _():
@@ -350,7 +354,7 @@
     f32, bf16 = jnp.float32, jnp.bfloat16
     sums = pl.pallas_call(
         functools.partial(kernel, groups, planes),
-        out_shape=jax.ShapeDtypeStruct((REACH, LAG_ROWS, chans), f32),
+        out_shape=jax.ShapeDtypeStruct((REACH, LAGS, chans), f32),
         in_specs=[hbm, vmem, hbm, vmem, vmem],
         out_specs=vmem,
         scratch_shapes=[
@@ -360,10 +364,8 @@
             pltpu.VMEM((2, 2, 4, rows, 2 * NF), bf16),
             pltpu.VMEM((4, 6, rows, 2 * NF), bf16),
             pltpu.VMEM((4, 4, rows, 2 * NF), bf16),
-            pltpu.VMEM((len(BIG) * 8, 2 * NF), f32),
-            pltpu.VMEM((len(SMALL) * 8, 2 * NF), f32),
-            pltpu.VMEM((4, len(BIG), 8, LAG_PAD), f32),
-            pltpu.VMEM((4, len(SMALL), 8, LAG_PAD), f32),
+            pltpu.VMEM(((len(BIG) + len(SMALL)) * 8, 2 * NF), f32),
+            pltpu.VMEM((4, len(BIG) + len(SMALL), 8, LAG_PAD), f32),
             pltpu.VMEM((planes, REACH, chans, LAG_PAD), f32),
             pltpu.SemaphoreType.DMA((8,)),
             pltpu.SemaphoreType.DMA,
@@ -389,7 +391,7 @@
     result = jnp.zeros((REACH, LAGS, chans), f32)
     for d in range(REACH):
         chosen = (owners == reader + d + 1)[:, None, None]
-        result = result + jnp.where(chosen, sums[d, :LAGS][None], jnp.float32(0))
+        result = result + jnp.where(chosen, sums[d][None], jnp.float32(0))
     return result[None]
 
 

time: 56.9 us -> 59 us (1.037)
  Pallas kernels: 54.9 us -> 57 us
    pallas_call x1, Pallas kernels: 54.9 us -> 57 us  [body(): pl.pallas_call(functools.partial(kernel, groups, planes), out_shape=jax.S...]
where the time goes in v2:
time: 59 us; the launch traced here: 58.8 us
  Pallas kernels  57 us (97%)
  local copies, waits for them, and re-layouts  0.91 us (2%)
  other arithmetic  0.89 us (2%)
    pallas_call x1, Pallas kernels, body(): pl.pallas_call(functools.partial(kernel, groups, planes), out_shape=jax.S...  57 us

profile of v2, /device:TPU:0, one launch (start us, length us, event | category | flops | bytes accessed | tf_op | source)
XLA Modules:
  0.0 58.8 jit_solution(9247426227024884785)
XLA Ops:
  0.0 0.0 copy-start
  0.0 57.0 %correlate.1 = f32[4,101,128]{2,1,0:T(8,128)} custom-call(bf16[24,128,1024]{2,1,0:T(8,128)(2,1)} %bitcast.18, s32[24,1024]{1,0:T(8,128)} %bitcast.19, bf16[1024,512]{1,0:T(8,128)(2,1)} %constant.24.clone.forward, bf16[512,256]{1,0:T(8,128)(2,1)} %constant.25.clone.smoother, bf16[1536,128]{1,0:T(8,128)(2,1)} %constant.26.clone.inverse), custom_call_target="tpu_custom_call" | custom-call | tf_op jit(solution)/shard_map/correlate/pallas_call | solution.py:355
  57.0 0.9 %slice_bitcast_fusion.3 = (f32[101,128]{1,0:T(8,128)S(1)}, f32[101,128]{1,0:T(8,128)S(1)}, f32[101,128]{1,0:T(8,128)S(1)}, f32[101,128]{1,0:T(8,128)S(1)}) fusion(f32[4,101,128]{2,1,0:T(8,128)} %correlate.1), kind=kLoop, calls=%fused_computation.4 | loop fusion | bytes 413696 | tf_op jit(solution)/shard_map/jit(_where)/broadcast_in_dim | solution.py:394
  57.9 0.0 copy-done
  57.9 0.9 %select_add_fusion = f32[1,4,101,128]{3,1,2,0:T(4,128)} fusion(f32[101,128]{1,0:T(8,128)S(1)} %get-tuple-element.6, f32[101,128]{1,0:T(8,128)S(1)} %get-tuple-element.7, f32[101,128]{1,0:T(8,128)S(1)} %get-tuple-element.8, f32[101,128]{1,0:T(8,128)S(1)} %get-tuple-element.5, pred[4]{0:T(512)(128)(4,1)S(1)} %get-tuple-element.11, ...), kind=kLoop, calls=%fused_computation | loop fusion | flops 361984 | bytes 413712 | tf_op jit(solution)/shard_map/add | solution.py:394
  (1 shorter events, 0.0 us)
Async XLA Ops:
  0.0 57.9 %copy-start = (s32[1,4]{1,0:T(1,128)S(1)}, s32[1,4]{1,0:T(1,128)}, u32[]{:S(2)}) copy-start(s32[1,4]{1,0:T(1,128)} %param.8) | copy-start | bytes 52

commit v3 on v2

--- a/solution.py
+++ b/solution.py
@@ -16,6 +16,7 @@
 SMOOTH = 4
 REACH = 4
 LAG_PAD = 128
+AHEAD = 4
 
 WATER = 0.05
 EPS = 1e-06
@@ -47,7 +48,12 @@
     table = np.pad(table, ((0, 0), (0, LAG_PAD - LAGS))).astype(np.float32)
     high = table.astype(ml_dtypes.bfloat16)
     low = (table - high.astype(np.float32)).astype(ml_dtypes.bfloat16)
-    return np.concatenate([high, high, low], axis=0)
+    tiles = NF // 128
+    parts = []
+    for f in range(tiles):
+        picked = np.concatenate([np.arange(f * 128, f * 128 + 128), np.arange(NF + f * 128, NF + f * 128 + 128)])
+        parts.append(np.concatenate([high[picked], high[picked], low[picked]], axis=0))
+    return np.stack(parts)
 
 
 def smooth_table():
@@ -58,13 +64,15 @@
 
 def kernel(
     groups, planes,
-    traces, mask, forward, smoother, inverse,
+    traces, mask, owners, forward, smoother_hbm, inverse_hbm,
     out,
-    tbuf, fbuf, maskx, own, big, small, cross_sum, res, rbuf,
+    tbuf, fbuf, smoother, inverse, maskx, own, big, small, cross_sum, res, rbuf,
     tsem, fsem, send_sem, big_sem, small_sem, rsend, rsem,
 ):
     wins = traces.shape[0]
     rows = own.shape[3]
+    tiles = NF // 128
+    pieces = 4 * tiles
     me = lax.axis_index("chan")
     tm = lax.axis_index("tm")
     core = lax.rem(me, 2)
@@ -87,8 +95,12 @@
         )
 
     load(0).start()
-    table_copy = pltpu.make_async_copy(forward, fbuf, fsem)
-    table_copy.start()
+    tables = [
+        pltpu.make_async_copy(source, target, fsem.at[n])
+        for n, (source, target) in enumerate(((forward, fbuf), (smoother_hbm, smoother), (inverse_hbm, inverse)))
+    ]
+    for table in tables:
+        table.start()
     for p in range(1, 8):
         load(p).start()
 
@@ -114,9 +126,9 @@
         row = mask[w : w + 1, :].astype(jnp.float32)
         maskx[w] = jnp.broadcast_to(row, (16, row.shape[1])).astype(jnp.bfloat16)
 
-    def chunk_copies(e, c, j, act, act_local):
-        src = own.at[e, c, j]
-        slot = (e * 2 + c) * 4 + j
+    def chunk_copies(e, c, q, act, act_local):
+        src = own.at[e, c, q]
+        slot = (e * 2 + c) * pieces + q
         is_big = e == y
         zt = z + 2 * e - 1
         has_z = (zt >= 0) & (zt < depth)
@@ -131,33 +143,33 @@
 
         @pl.when(is_big & has_z)
         def _():
-            remote(big.at[j, 4 * (1 - y) + core], 0, big_sem.at[j], zt * 4 + y * 2 + c)
+            remote(big.at[q, 4 * (1 - y) + core], 0, big_sem.at[q], zt * 4 + y * 2 + c)
 
         @pl.when(jnp.logical_not(is_big))
         def _():
-            remote(big.at[j, 2 + core], 1, big_sem.at[j], z * 4 + (1 - y) * 2 + c)
+            remote(big.at[q, 2 + core], 1, big_sem.at[q], z * 4 + (1 - y) * 2 + c)
 
         @pl.when(jnp.logical_not(is_big) & has_z)
         def _():
-            remote(small.at[j, 2 * (1 - e) + core], 0, small_sem.at[j], zt * 4 + y * 2 + c)
+            remote(small.at[q, 2 * (1 - e) + core], 0, small_sem.at[q], zt * 4 + y * 2 + c)
 
         @pl.when(is_big & (c != core))
         def _():
-            remote(big.at[j, 4 * y + core], 2, big_sem.at[j], z * 4 + y * 2 + c)
+            remote(big.at[q, 4 * y + core], 2, big_sem.at[q], z * 4 + y * 2 + c)
 
         @pl.when(jnp.logical_not(is_big) & has_small & (c != core))
         def _():
-            remote(small.at[j, 2 * (1 - y) + core], 2, small_sem.at[j], z * 4 + y * 2 + c)
+            remote(small.at[q, 2 * (1 - y) + core], 2, small_sem.at[q], z * 4 + y * 2 + c)
 
         if act_local:
 
             @pl.when(is_big & (c == core))
             def _():
-                pltpu.make_async_copy(src, big.at[j, 4 * y + core], big_sem.at[j]).start()
+                pltpu.make_async_copy(src, big.at[q, 4 * y + core], big_sem.at[q]).start()
 
             @pl.when(jnp.logical_not(is_big) & has_small & (c == core))
             def _():
-                pltpu.make_async_copy(src, small.at[j, 2 * (1 - y) + core], small_sem.at[j]).start()
+                pltpu.make_async_copy(src, small.at[q, 2 * (1 - y) + core], small_sem.at[q]).start()
 
     def start(copy):
         copy.start()
@@ -165,7 +177,8 @@
     def wait_send(copy):
         copy.wait_send()
 
-    table_copy.wait()
+    for table in tables:
+        table.wait()
 
     def produce(p, carry):
         e = lax.rem(p, 2)
@@ -181,57 +194,53 @@
         both = jnp.concatenate([amplitude.astype(jnp.bfloat16), scaled.astype(jnp.bfloat16)], axis=1)
         total = jnp.dot(both, smoother[...], preferred_element_type=jnp.float32)
         gain = jnp.float32(2 * SMOOTH + 1) / (total + jnp.float32((2 * SMOOTH + 1) * EPS))
-        for part, lo in ((real, 0), (imag, NF)):
+        for n, part in enumerate((real, imag)):
             white = (part * gain).reshape(wins, 16, NF)
             for h in range(2):
-                own[e, c, 2 * half + h, :, lo : lo + NF] = (
-                    white[:, 8 * h : 8 * h + 8, :].reshape(wins * 8, NF).astype(jnp.bfloat16)
-                )
+                for f in range(tiles):
+                    own[e, c, (2 * half + h) * tiles + f, :, n * 128 : n * 128 + 128] = (
+                        white[:, 8 * h : 8 * h + 8, f * 128 : f * 128 + 128]
+                        .reshape(wins * 8, 128)
+                        .astype(jnp.bfloat16)
+                    )
 
         @pl.when(p == 0)
         def _():
             pl.semaphore_wait(barrier, partners)
 
-        chunk_copies(e, c, half, start, True)
+        for n in range(AHEAD // 2):
+            chunk_copies(e, c, half * (AHEAD // 2) + n, start, True)
         return carry
 
     lax.fori_loop(0, 8, produce, 0)
 
-    def send_rest(n, carry):
-        chunk_copies(lax.rem(n, 2), lax.rem(n // 2, 2), 2 + n // 4, start, True)
-        return carry
-
-    lax.fori_loop(0, 8, send_rest, 0)
-
-    def cross(buf, j, pairs, first):
+    def cross(buf, q, pairs, first):
         used = sorted({s for pair in pairs for s in pair})
-        for f in range(NF // 128):
-            lo = f * 128
-
-            def step(i, sums):
-                r = pl.ds(pl.multiple_of(i * 16, 16), 16)
-                re = {s: buf[j, s, r, lo : lo + 128].astype(jnp.float32) for s in used}
-                im = {s: buf[j, s, r, NF + lo : NF + lo + 128].astype(jnp.float32) for s in used}
-                new = []
-                for n, (a, b) in enumerate(pairs):
-                    direct = re[a] * re[b] + im[a] * im[b]
-                    crossed = re[a] * im[b] - im[a] * re[b]
-                    new.append(sums[2 * n] + (direct[:8] + direct[8:]))
-                    new.append(sums[2 * n + 1] + (crossed[:8] + crossed[8:]))
-                return tuple(new)
-
-            zero = jnp.zeros((8, 128), jnp.float32)
-            sums = lax.fori_loop(0, rows // 16, step, (zero,) * (2 * len(pairs)))
-            for n in range(len(pairs)):
-                cross_sum[first + 8 * n : first + 8 * n + 8, lo : lo + 128] = sums[2 * n]
-                cross_sum[first + 8 * n : first + 8 * n + 8, NF + lo : NF + lo + 128] = sums[2 * n + 1]
-
-    def lags():
+
+        def step(i, sums):
+            r = pl.ds(pl.multiple_of(i * 16, 16), 16)
+            re = {s: buf[q, s, r, 0:128].astype(jnp.float32) for s in used}
+            im = {s: buf[q, s, r, 128:256].astype(jnp.float32) for s in used}
+            new = []
+            for n, (a, b) in enumerate(pairs):
+                direct = re[a] * re[b] + im[a] * im[b]
+                crossed = re[a] * im[b] - im[a] * re[b]
+                new.append(sums[2 * n] + (direct[:8] + direct[8:]))
+                new.append(sums[2 * n + 1] + (crossed[:8] + crossed[8:]))
+            return tuple(new)
+
+        zero = jnp.zeros((8, 128), jnp.float32)
+        sums = lax.fori_loop(0, rows // 16, step, (zero,) * (2 * len(pairs)))
+        for n in range(len(pairs)):
+            cross_sum[first + 8 * n : first + 8 * n + 8, 0:128] = sums[2 * n]
+            cross_sum[first + 8 * n : first + 8 * n + 8, 128:256] = sums[2 * n + 1]
+
+    def lags(f):
         value = cross_sum[...]
         high = value.astype(jnp.bfloat16)
         low = (value - high.astype(jnp.float32)).astype(jnp.bfloat16)
         return jnp.dot(
-            jnp.concatenate([high, low, high], axis=1), inverse[...], preferred_element_type=jnp.float32
+            jnp.concatenate([high, low, high], axis=1), inverse[f], preferred_element_type=jnp.float32
         ).reshape(-1, 8, LAG_PAD)
 
     def messages(j, base, e, first, listed, act, act_local):
@@ -282,45 +291,64 @@
         def _():
             messages(j, small_base, 1 - y, 5, [(0, 14, 1, 3), (1, 15, 2, 2)], act, act_local)
 
-    def correlate(j, carry):
+    def correlate(q, carry):
+        j = q // tiles
+        f = lax.rem(q, tiles)
+
         @pl.when(has_small)
         def _():
-            pltpu.make_async_copy(small.at[j], small.at[j], small_sem.at[j]).wait()
+            pltpu.make_async_copy(small.at[q], small.at[q], small_sem.at[q]).wait()
 
         @pl.when(has_big)
         def _():
-            pltpu.make_async_copy(big.at[j], big.at[j], big_sem.at[j]).wait()
+            pltpu.make_async_copy(big.at[q], big.at[q], big_sem.at[q]).wait()
 
         @pl.when(jnp.logical_not(has_big))
         def _():
-            there = big.at[j, pl.ds(2 * y, 4)]
-            pltpu.make_async_copy(there, there, big_sem.at[j]).wait()
-
-        @pl.when(j > 0)
+            there = big.at[q, pl.ds(2 * y, 4)]
+            pltpu.make_async_copy(there, there, big_sem.at[q]).wait()
+
+        @pl.when(q < pieces - AHEAD)
+        def _():
+            for c in range(2):
+                for e in range(2):
+                    chunk_copies(e, c, q + AHEAD, start, True)
+
+        cross(big, q, BIG, 0)
+
+        @pl.when(has_small)
+        def _():
+            cross(small, q, SMALL, 8 * len(BIG))
+
+        @pl.when(f == 0)
+        def _():
+            res[j] = lags(f)
+
+        @pl.when(f > 0)
+        def _():
+            res[j] += lags(f)
+
+        @pl.when((f == tiles - 1) & (j > 0))
         def _():
             big_messages(j - 1, wait_send, False)
             small_messages(j - 1, wait_send, False)
 
-        cross(big, j, BIG, 0)
-
-        @pl.when(has_small)
-        def _():
-            cross(small, j, SMALL, 8 * len(BIG))
-
-        res[j] = lags()
-        big_messages(j, start, True)
-        small_messages(j, start, True)
+        @pl.when(f == tiles - 1)
+        def _():
+            big_messages(j, start, True)
+            small_messages(j, start, True)
+
         return carry
 
-    lax.fori_loop(0, 4, correlate, 0)
+    lax.fori_loop(0, pieces, correlate, 0)
     big_messages(3, wait_send, False)
     small_messages(3, wait_send, False)
 
     def drain(n, carry):
-        chunk_copies(n // 8, lax.rem(n // 4, 2), lax.rem(n, 4), wait_send, False)
+        chunk_copies(n // (2 * pieces), lax.rem(n // pieces, 2), lax.rem(n, pieces), wait_send, False)
         return carry
 
-    lax.fori_loop(0, 16, drain, 0)
+    lax.fori_loop(0, 4 * pieces, drain, 0)
 
     valid = jnp.minimum(REACH, groups - 1 - me)
     for n in range(1, REACH + 1):
@@ -330,18 +358,18 @@
             whole = rbuf.at[:, pl.ds(0, n)]
             pltpu.make_async_copy(whole, whole, rsem).wait()
 
+    parts = []
     for d in range(REACH):
-
-        @pl.when(d < valid)
-        def _():
-            total = rbuf[0, d]
-            for t in range(1, planes):
-                total = total + rbuf[t, d]
-            out[d] = total.T[:LAGS]
-
-        @pl.when(d >= valid)
-        def _():
-            out[d] = jnp.zeros(out.shape[1:], jnp.float32)
+        total = rbuf[0, d]
+        for t in range(1, planes):
+            total = total + rbuf[t, d]
+        parts.append(total.T[:LAGS])
+    for p in range(REACH):
+        owner = jnp.full(parts[0].shape, owners[0, p], jnp.int32)
+        picked = jnp.zeros(parts[0].shape, jnp.float32)
+        for d in range(REACH):
+            picked = jnp.where(owner == me + (d + 1), parts[d], picked)
+        out[p] = picked
 
 
 def body(traces, valid_mask, pair_owner):
@@ -349,29 +377,33 @@
     groups = lax.axis_size("chan")
     planes = lax.axis_size("tm")
     rows = wins * 8
+    tiles = NF // 128
+    pieces = 4 * tiles
     vmem = pl.BlockSpec(memory_space=pltpu.VMEM)
     hbm = pl.BlockSpec(memory_space=pl.ANY)
     f32, bf16 = jnp.float32, jnp.bfloat16
-    sums = pl.pallas_call(
+    result = pl.pallas_call(
         functools.partial(kernel, groups, planes),
         out_shape=jax.ShapeDtypeStruct((REACH, LAGS, chans), f32),
-        in_specs=[hbm, vmem, hbm, vmem, vmem],
+        in_specs=[hbm, vmem, pl.BlockSpec(memory_space=pltpu.SMEM), hbm, hbm, hbm],
         out_specs=vmem,
         scratch_shapes=[
             pltpu.VMEM((8, wins, 16, samples), bf16),
             pltpu.VMEM((samples, 2 * NF), bf16),
+            pltpu.VMEM((2 * NF, NF), bf16),
+            pltpu.VMEM((tiles, 3 * 256, LAG_PAD), bf16),
             pltpu.VMEM((wins, 16, samples), bf16),
-            pltpu.VMEM((2, 2, 4, rows, 2 * NF), bf16),
-            pltpu.VMEM((4, 6, rows, 2 * NF), bf16),
-            pltpu.VMEM((4, 4, rows, 2 * NF), bf16),
-            pltpu.VMEM(((len(BIG) + len(SMALL)) * 8, 2 * NF), f32),
+            pltpu.VMEM((2, 2, pieces, rows, 256), bf16),
+            pltpu.VMEM((pieces, 6, rows, 256), bf16),
+            pltpu.VMEM((pieces, 4, rows, 256), bf16),
+            pltpu.VMEM(((len(BIG) + len(SMALL)) * 8, 256), f32),
             pltpu.VMEM((4, len(BIG) + len(SMALL), 8, LAG_PAD), f32),
             pltpu.VMEM((planes, REACH, chans, LAG_PAD), f32),
             pltpu.SemaphoreType.DMA((8,)),
-            pltpu.SemaphoreType.DMA,
-            pltpu.SemaphoreType.DMA((16, 3)),
-            pltpu.SemaphoreType.DMA((4,)),
-            pltpu.SemaphoreType.DMA((4,)),
+            pltpu.SemaphoreType.DMA((3,)),
+            pltpu.SemaphoreType.DMA((4 * pieces, 3)),
+            pltpu.SemaphoreType.DMA((pieces,)),
+            pltpu.SemaphoreType.DMA((pieces,)),
             pltpu.SemaphoreType.DMA((7, planes)),
             pltpu.SemaphoreType.DMA,
         ],
@@ -382,16 +414,11 @@
     )(
         traces[0],
         valid_mask[0],
+        pair_owner,
         jnp.asarray(forward_table(samples)),
         jnp.asarray(smooth_table()),
         jnp.asarray(inverse_table(samples, wins * planes)),
     )
-    reader = lax.axis_index("chan")
-    owners = pair_owner[0]
-    result = jnp.zeros((REACH, LAGS, chans), f32)
-    for d in range(REACH):
-        chosen = (owners == reader + d + 1)[:, None, None]
-        result = result + jnp.where(chosen, sums[d][None], jnp.float32(0))
     return result[None]
 
 

time: 59 us -> 54 us (0.915)
  Pallas kernels: 57 us -> 52.1 us
  other arithmetic: 0.89 us -> 0 us
  local copies, waits for them, and re-layouts: 0.91 us -> 1.67 us
    pallas_call x1, Pallas kernels: 57 us -> 52.1 us  [body(): pl.pallas_call(functools.partial(kernel, groups, planes), out_shape=jax.S...]
    add x1 -> x0, other arithmetic: 0.88 us -> none  [body(): result = result + jnp.where(chosen, sums[d][None], jnp.float32(0))]
    broadcast_in_dim x1, local copies, waits for them, and re-layouts: 0.9 us -> 1.67 us  [body(): return result[None]]
where the time goes in v3:
time: 54 us; the launch traced here: 53.8 us
  Pallas kernels  52.1 us (96%)
  local copies, waits for them, and re-layouts  1.67 us (3%)
    pallas_call x1, Pallas kernels, body(): pl.pallas_call(functools.partial(kernel, groups, planes), out_shape=jax.S...  52.1 us
    broadcast_in_dim x1, local copies, waits for them, and re-layouts, body(): return result[None]  1.67 us

profile of v3, /device:TPU:0, one launch (start us, length us, event | category | flops | bytes accessed | tf_op | source)
XLA Modules:
  0.0 53.8 jit_solution(9773309496513694999)
XLA Ops:
  0.0 52.1 %correlate.1 = f32[4,101,128]{2,1,0:T(8,128)} custom-call(bf16[24,128,1024]{2,1,0:T(8,128)(2,1)} %bitcast.3, s32[24,1024]{1,0:T(8,128)} %bitcast.5, s32[1,4]{1,0:T(1,128)} %owners.1, bf16[1024,512]{1,0:T(8,128)(2,1)} %constant.6.clone.forward, bf16[512,256]{1,0:T(8,128)(2,1)} %constant.7.clone.smoother_hbm, bf16[2,768,128]{2,1,0:T(8,128)(2,1)} %constant.8.clone.inverse_hbm), custom_call_target="tpu_custom_call" | custom-call | tf_op jit(solution)/shard_map/correlate/pallas_call | solution.py:385
  52.1 1.7 %copy.7 = f32[1,4,101,128]{3,1,2,0:T(4,128)} copy(f32[1,4,101,128]{3,2,1,0:T(8,128)} %bitcast.4) | data formatting | bytes 413696 | tf_op jit(solution)/shard_map/broadcast_in_dim | solution.py:422

commit v4 on v3

--- a/solution.py
+++ b/solution.py
@@ -66,7 +66,7 @@
     groups, planes,
     traces, mask, owners, forward, smoother_hbm, inverse_hbm,
     out,
-    tbuf, fbuf, smoother, inverse, maskx, own, big, small, cross_sum, res, rbuf,
+    tbuf, fbuf, smoother, inverse, maskx, own, big, small, cross_sum, res, packed, rbuf,
     tsem, fsem, send_sem, big_sem, small_sem, rsend, rsem,
 ):
     wins = traces.shape[0]
@@ -244,10 +244,10 @@
         ).reshape(-1, 8, LAG_PAD)
 
     def messages(j, base, e, first, listed, act, act_local):
-        at = pl.ds(pl.multiple_of(e * 64 + core * 32 + j * 8, 8), 8)
+        at = pl.ds(pl.multiple_of(e * 64 + core * 32 + j * 16, 16), 16)
         for k, (s, pair, count, distance) in enumerate(listed):
             chan = base + s
-            src = res.at[j, pl.ds(pair, count)]
+            src = packed.at[j, pl.ds(pair, count)]
             dst = rbuf.at[tm, pl.ds(distance, count), at]
             for t in range(planes):
                 mine = (chan == me) & (t == tm)
@@ -320,29 +320,34 @@
         def _():
             cross(small, q, SMALL, 8 * len(BIG))
 
+        h = lax.rem(j, 2)
+
         @pl.when(f == 0)
         def _():
-            res[j] = lags(f)
+            res[h] = lags(f)
 
         @pl.when(f > 0)
         def _():
-            res[j] += lags(f)
-
-        @pl.when((f == tiles - 1) & (j > 0))
-        def _():
-            big_messages(j - 1, wait_send, False)
-            small_messages(j - 1, wait_send, False)
-
-        @pl.when(f == tiles - 1)
-        def _():
-            big_messages(j, start, True)
-            small_messages(j, start, True)
+            res[h] += lags(f)
+
+        last = (f == tiles - 1) & (h == 1)
+
+        @pl.when(last & (j > 1))
+        def _():
+            big_messages(0, wait_send, False)
+            small_messages(0, wait_send, False)
+
+        @pl.when(last)
+        def _():
+            packed[j // 2] = jnp.concatenate([res[0], res[1]], axis=1).astype(jnp.bfloat16)
+            big_messages(j // 2, start, True)
+            small_messages(j // 2, start, True)
 
         return carry
 
     lax.fori_loop(0, pieces, correlate, 0)
-    big_messages(3, wait_send, False)
-    small_messages(3, wait_send, False)
+    big_messages(1, wait_send, False)
+    small_messages(1, wait_send, False)
 
     def drain(n, carry):
         chunk_copies(n // (2 * pieces), lax.rem(n // pieces, 2), lax.rem(n, pieces), wait_send, False)
@@ -360,16 +365,16 @@
 
     parts = []
     for d in range(REACH):
-        total = rbuf[0, d]
+        total = rbuf[0, d].astype(jnp.float32)
         for t in range(1, planes):
-            total = total + rbuf[t, d]
+            total = total + rbuf[t, d].astype(jnp.float32)
         parts.append(total.T[:LAGS])
     for p in range(REACH):
         owner = jnp.full(parts[0].shape, owners[0, p], jnp.int32)
         picked = jnp.zeros(parts[0].shape, jnp.float32)
         for d in range(REACH):
             picked = jnp.where(owner == me + (d + 1), parts[d], picked)
-        out[p] = picked
+        out[:, p, :] = picked
 
 
 def body(traces, valid_mask, pair_owner):
@@ -384,7 +389,7 @@
     f32, bf16 = jnp.float32, jnp.bfloat16
     result = pl.pallas_call(
         functools.partial(kernel, groups, planes),
-        out_shape=jax.ShapeDtypeStruct((REACH, LAGS, chans), f32),
+        out_shape=jax.ShapeDtypeStruct((LAGS, REACH, chans), f32),
         in_specs=[hbm, vmem, pl.BlockSpec(memory_space=pltpu.SMEM), hbm, hbm, hbm],
         out_specs=vmem,
         scratch_shapes=[
@@ -397,8 +402,9 @@
             pltpu.VMEM((pieces, 6, rows, 256), bf16),
             pltpu.VMEM((pieces, 4, rows, 256), bf16),
             pltpu.VMEM(((len(BIG) + len(SMALL)) * 8, 256), f32),
-            pltpu.VMEM((4, len(BIG) + len(SMALL), 8, LAG_PAD), f32),
-            pltpu.VMEM((planes, REACH, chans, LAG_PAD), f32),
+            pltpu.VMEM((2, len(BIG) + len(SMALL), 8, LAG_PAD), f32),
+            pltpu.VMEM((2, len(BIG) + len(SMALL), 16, LAG_PAD), bf16),
+            pltpu.VMEM((planes, REACH, chans, LAG_PAD), bf16),
             pltpu.SemaphoreType.DMA((8,)),
             pltpu.SemaphoreType.DMA((3,)),
             pltpu.SemaphoreType.DMA((4 * pieces, 3)),
@@ -419,7 +425,7 @@
         jnp.asarray(smooth_table()),
         jnp.asarray(inverse_table(samples, wins * planes)),
     )
-    return result[None]
+    return result.transpose(1, 0, 2)[None]
 
 
 def solution(mesh):

time: 54 us -> 51.6 us (0.956)
  Pallas kernels: 52.1 us -> 49.8 us
    pallas_call x1, Pallas kernels: 52.1 us -> 49.8 us  [body(): pl.pallas_call(functools.partial(kernel, groups, planes), out_shape=jax.S...]
    broadcast_in_dim x1 -> x0, local copies, waits for them, and re-layouts: 1.67 us -> none  [body(): return result[None]]
    unnamed x0 -> x1, local copies, waits for them, and re-layouts: none -> 1.63 us
where the time goes in v4:
time: 51.6 us; the launch traced here: 51.4 us
  Pallas kernels  49.8 us (97%)
  local copies, waits for them, and re-layouts  1.63 us (3%)
    pallas_call x1, Pallas kernels, body(): pl.pallas_call(functools.partial(kernel, groups, planes), out_shape=jax.S...  49.8 us
    unnamed x1, local copies, waits for them, and re-layouts  1.63 us

profile of v4, /device:TPU:0, one launch (start us, length us, event | category | flops | bytes accessed | tf_op | source)
XLA Modules:
  0.0 51.4 jit_solution(13579106611702329621)
XLA Ops:
  0.0 49.8 %correlate.1 = f32[101,4,128]{2,1,0:T(4,128)} custom-call(bf16[24,128,1024]{2,1,0:T(8,128)(2,1)} %bitcast.5, s32[24,1024]{1,0:T(8,128)} %bitcast.7, s32[1,4]{1,0:T(1,128)} %owners.1, bf16[1024,512]{1,0:T(8,128)(2,1)} %constant.6.clone.forward, bf16[512,256]{1,0:T(8,128)(2,1)} %constant.7.clone.smoother_hbm, bf16[2,768,128]{2,1,0:T(8,128)(2,1)} %constant.8.clone.inverse_hbm), custom_call_target="tpu_custom_call" | custom-call | tf_op jit(solution)/shard_map/correlate/pallas_call | solution.py:390
  49.8 1.6 %copy.8 = f32[1,4,101,128]{3,1,2,0:T(4,128)} copy(f32[1,4,101,128]{3,1,2,0:T(4,128)} %bitcast.6) | data formatting | bytes 413696

commit v5 on v4

--- a/solution.py
+++ b/solution.py
@@ -16,7 +16,7 @@
 SMOOTH = 4
 REACH = 4
 LAG_PAD = 128
-AHEAD = 4
+AHEAD = 2
 
 WATER = 0.05
 EPS = 1e-06

time: 51.6 us -> 52 us (level)
  no operation moved by 1% of the time
where the time goes in v5:
time: 52 us; the launch traced here: 51.9 us
  Pallas kernels  50.2 us (97%)
  local copies, waits for them, and re-layouts  1.63 us (3%)
    pallas_call x1, Pallas kernels, body(): pl.pallas_call(functools.partial(kernel, groups, planes), out_shape=jax.S...  50.2 us
    unnamed x1, local copies, waits for them, and re-layouts  1.63 us

profile of v5, /device:TPU:0, one launch (start us, length us, event | category | flops | bytes accessed | tf_op | source)
XLA Modules:
  0.0 51.9 jit_solution(12120598891400842327)
XLA Ops:
  0.0 50.2 %correlate.1 = f32[101,4,128]{2,1,0:T(4,128)} custom-call(bf16[24,128,1024]{2,1,0:T(8,128)(2,1)} %bitcast.5, s32[24,1024]{1,0:T(8,128)} %bitcast.7, s32[1,4]{1,0:T(1,128)} %owners.1, bf16[1024,512]{1,0:T(8,128)(2,1)} %constant.6.clone.forward, bf16[512,256]{1,0:T(8,128)(2,1)} %constant.7.clone.smoother_hbm, bf16[2,768,128]{2,1,0:T(8,128)(2,1)} %constant.8.clone.inverse_hbm), custom_call_target="tpu_custom_call" | custom-call | tf_op jit(solution)/shard_map/correlate/pallas_call | solution.py:390
  50.2 1.6 %copy.8 = f32[1,4,101,128]{3,1,2,0:T(4,128)} copy(f32[1,4,101,128]{3,1,2,0:T(4,128)} %bitcast.6) | data formatting | bytes 413696

commit v6 on v4

--- a/solution.py
+++ b/solution.py
@@ -64,9 +64,9 @@
 
 def kernel(
     groups, planes,
-    traces, mask, owners, forward, smoother_hbm, inverse_hbm,
+    traces, mask_hbm, owners, forward, smoother_hbm, inverse_hbm,
     out,
-    tbuf, fbuf, smoother, inverse, maskx, own, big, small, cross_sum, res, packed, rbuf,
+    mask, tbuf, fbuf, smoother, inverse, maskx, own, big, small, cross_sum, res, packed, rbuf,
     tsem, fsem, send_sem, big_sem, small_sem, rsend, rsem,
 ):
     wins = traces.shape[0]
@@ -94,15 +94,17 @@
             traces.at[:, pl.ds(pl.multiple_of(channel_start(p), 16), 16), :], tbuf.at[p], tsem.at[p]
         )
 
-    load(0).start()
     tables = [
         pltpu.make_async_copy(source, target, fsem.at[n])
-        for n, (source, target) in enumerate(((forward, fbuf), (smoother_hbm, smoother), (inverse_hbm, inverse)))
+        for n, (source, target) in enumerate(
+            ((mask_hbm, mask), (forward, fbuf), (smoother_hbm, smoother), (inverse_hbm, inverse))
+        )
     ]
-    for table in tables:
-        table.start()
-    for p in range(1, 8):
-        load(p).start()
+    tables[0].start()
+    load(0).start()
+    tables[1].start()
+    tables[2].start()
+    load(1).start()
 
     barrier = pltpu.get_barrier_semaphore()
     for dz in (-1, 0, 1):
@@ -122,6 +124,7 @@
     near = 1 + has_up.astype(jnp.int32) + has_down.astype(jnp.int32)
     partners = near * (4 * planes) - 1
 
+    tables[0].wait()
     for w in range(wins):
         row = mask[w : w + 1, :].astype(jnp.float32)
         maskx[w] = jnp.broadcast_to(row, (16, row.shape[1])).astype(jnp.bfloat16)
@@ -177,14 +180,20 @@
     def wait_send(copy):
         copy.wait_send()
 
-    for table in tables:
-        table.wait()
+    tables[1].wait()
+    tables[2].wait()
+    tables[3].start()
 
     def produce(p, carry):
         e = lax.rem(p, 2)
         c = lax.rem(p // 2, 2)
         half = p // 4
         load(p).wait()
+
+        @pl.when(p < 6)
+        def _():
+            load(p + 2).start()
+
         x = (tbuf[p] * maskx[...]).reshape(wins * 16, tbuf.shape[3])
         spectra = jnp.dot(x, fbuf[...], preferred_element_type=jnp.float32)
         real = spectra[:, :NF]
@@ -213,6 +222,7 @@
         return carry
 
     lax.fori_loop(0, 8, produce, 0)
+    tables[3].wait()
 
     def cross(buf, q, pairs, first):
         used = sorted({s for pair in pairs for s in pair})
@@ -298,6 +308,7 @@
         @pl.when(has_small)
         def _():
             pltpu.make_async_copy(small.at[q], small.at[q], small_sem.at[q]).wait()
+            cross(small, q, SMALL, 8 * len(BIG))
 
         @pl.when(has_big)
         def _():
@@ -315,10 +326,6 @@
                     chunk_copies(e, c, q + AHEAD, start, True)
 
         cross(big, q, BIG, 0)
-
-        @pl.when(has_small)
-        def _():
-            cross(small, q, SMALL, 8 * len(BIG))
 
         h = lax.rem(j, 2)
 
@@ -390,9 +397,10 @@
     result = pl.pallas_call(
         functools.partial(kernel, groups, planes),
         out_shape=jax.ShapeDtypeStruct((LAGS, REACH, chans), f32),
-        in_specs=[hbm, vmem, pl.BlockSpec(memory_space=pltpu.SMEM), hbm, hbm, hbm],
+        in_specs=[hbm, hbm, pl.BlockSpec(memory_space=pltpu.SMEM), hbm, hbm, hbm],
         out_specs=vmem,
         scratch_shapes=[
+            pltpu.VMEM((wins, samples), jnp.int32),
             pltpu.VMEM((8, wins, 16, samples), bf16),
             pltpu.VMEM((samples, 2 * NF), bf16),
             pltpu.VMEM((2 * NF, NF), bf16),
@@ -406,7 +414,7 @@
             pltpu.VMEM((2, len(BIG) + len(SMALL), 16, LAG_PAD), bf16),
             pltpu.VMEM((planes, REACH, chans, LAG_PAD), bf16),
             pltpu.SemaphoreType.DMA((8,)),
-            pltpu.SemaphoreType.DMA((3,)),
+            pltpu.SemaphoreType.DMA((4,)),
             pltpu.SemaphoreType.DMA((4 * pieces, 3)),
             pltpu.SemaphoreType.DMA((pieces,)),
             pltpu.SemaphoreType.DMA((pieces,)),
@@ -425,6 +433,8 @@
         jnp.asarray(smooth_table()),
         jnp.asarray(inverse_table(samples, wins * planes)),
     )
+    held = pair_owner[0] >= 0
+    result = jnp.where(held[None, :, None], result, jnp.float32(0))
     return result.transpose(1, 0, 2)[None]
 
 

time: 51.6 us -> 50.7 us (0.983)
  other arithmetic: 0 us -> 2.38 us
  Pallas kernels: 49.8 us -> 48.1 us
  local copies, waits for them, and re-layouts: 1.63 us -> 0 us
    broadcast_in_dim x0 -> x1, other arithmetic: none -> 1.72 us  [body(): return result.transpose(1, 0, 2)[None]]
    pallas_call x1, Pallas kernels: 49.8 us -> 48.1 us  [body(): pl.pallas_call(functools.partial(kernel, groups, planes), out_shape=jax.S...]
    unnamed x1 -> x0, local copies, waits for them, and re-layouts: 1.63 us -> none
    ge x0 -> x1, other arithmetic: none -> 0.66 us  [body(): held = pair_owner[0] >= 0]
where the time goes in v6:
time: 50.7 us; the launch traced here: 50.5 us
  Pallas kernels  48.1 us (95%)
  other arithmetic  2.38 us (5%)
    pallas_call x1, Pallas kernels, body(): pl.pallas_call(functools.partial(kernel, groups, planes), out_shape=jax.S...  48.1 us
    broadcast_in_dim x1, other arithmetic, body(): return result.transpose(1, 0, 2)[None]  1.72 us

profile of v6, /device:TPU:0, one launch (start us, length us, event | category | flops | bytes accessed | tf_op | source)
XLA Modules:
  0.0 50.5 jit_solution(16674141923729741446)
XLA Ops:
  0.0 0.7 %compare_bitcast_fusion = pred[4]{0:T(512)(128)(4,1)S(1)} fusion(s32[1,4]{1,0:T(1,128)} %owners.1), kind=kLoop, calls=%fused_computation.1 | loop fusion | flops 4 | bytes 20 | tf_op jit(solution)/shard_map/ge | solution.py:436
  0.7 48.1 %correlate.1 = f32[101,4,128]{2,1,0:T(4,128)} custom-call(bf16[24,128,1024]{2,1,0:T(8,128)(2,1)} %bitcast.8, s32[24,1024]{1,0:T(8,128)} %bitcast.9, s32[1,4]{1,0:T(1,128)} %owners.1, bf16[1024,512]{1,0:T(8,128)(2,1)} %constant.10.clone.forward, bf16[512,256]{1,0:T(8,128)(2,1)} %constant.11.clone.smoother_hbm, bf16[2,768,128]{2,1,0:T(8,128)(2,1)} %constant.12.clone.inverse_hbm), custom_call_target="tpu_custom_call" | custom-call | tf_op jit(solution)/shard_map/correlate/pallas_call | solution.py:397
  48.8 1.7 %select_bitcast_fusion = f32[1,4,101,128]{3,1,2,0:T(4,128)} fusion(f32[101,4,128]{2,1,0:T(4,128)} %correlate.1, pred[4]{0:T(512)(128)(4,1)S(1)} %compare_bitcast_fusion), kind=kLoop, calls=%fused_computation | loop fusion | flops 51712 | bytes 413700 | tf_op jit(solution)/shard_map/broadcast_in_dim | solution.py:438

commit v7 on v6

--- a/solution.py
+++ b/solution.py
@@ -168,11 +168,11 @@
 
             @pl.when(is_big & (c == core))
             def _():
-                pltpu.make_async_copy(src, big.at[q, 4 * y + core], big_sem.at[q]).start()
+                big[q, 4 * y + core] = src[...]
 
             @pl.when(jnp.logical_not(is_big) & has_small & (c == core))
             def _():
-                pltpu.make_async_copy(src, small.at[q, 2 * (1 - y) + core], small_sem.at[q]).start()
+                small[q, 2 * (1 - y) + core] = src[...]
 
     def start(copy):
         copy.start()
@@ -307,16 +307,18 @@
 
         @pl.when(has_small)
         def _():
-            pltpu.make_async_copy(small.at[q], small.at[q], small_sem.at[q]).wait()
+            there = small.at[q, pl.ds(0, 3)]
+            pltpu.make_async_copy(there, there, small_sem.at[q]).wait()
             cross(small, q, SMALL, 8 * len(BIG))
 
         @pl.when(has_big)
         def _():
-            pltpu.make_async_copy(big.at[q], big.at[q], big_sem.at[q]).wait()
+            there = big.at[q, pl.ds(0, 5)]
+            pltpu.make_async_copy(there, there, big_sem.at[q]).wait()
 
         @pl.when(jnp.logical_not(has_big))
         def _():
-            there = big.at[q, pl.ds(2 * y, 4)]
+            there = big.at[q, pl.ds(2 * y, 3)]
             pltpu.make_async_copy(there, there, big_sem.at[q]).wait()
 
         @pl.when(q < pieces - AHEAD)
@@ -381,7 +383,7 @@
         picked = jnp.zeros(parts[0].shape, jnp.float32)
         for d in range(REACH):
             picked = jnp.where(owner == me + (d + 1), parts[d], picked)
-        out[:, p, :] = picked
+        out[pl.ds(p, LAGS, REACH), :] = picked
 
 
 def body(traces, valid_mask, pair_owner):
@@ -396,7 +398,7 @@
     f32, bf16 = jnp.float32, jnp.bfloat16
     result = pl.pallas_call(
         functools.partial(kernel, groups, planes),
-        out_shape=jax.ShapeDtypeStruct((LAGS, REACH, chans), f32),
+        out_shape=jax.ShapeDtypeStruct((LAGS * REACH, chans), f32),
         in_specs=[hbm, hbm, pl.BlockSpec(memory_space=pltpu.SMEM), hbm, hbm, hbm],
         out_specs=vmem,
         scratch_shapes=[
@@ -433,9 +435,7 @@
         jnp.asarray(smooth_table()),
         jnp.asarray(inverse_table(samples, wins * planes)),
     )
-    held = pair_owner[0] >= 0
-    result = jnp.where(held[None, :, None], result, jnp.float32(0))
-    return result.transpose(1, 0, 2)[None]
+    return result.reshape(LAGS, REACH, chans).transpose(1, 0, 2)[None]
 
 
 def solution(mesh):

time: 50.7 us -> 49.9 us (0.984)
  other arithmetic: 2.38 us -> 0 us
  local copies, waits for them, and re-layouts: 0 us -> 1.67 us
    broadcast_in_dim x1 -> x0, other arithmetic: 1.72 us -> none  [body(): return result.transpose(1, 0, 2)[None]]
    reshape x0 -> x1, local copies, waits for them, and re-layouts: none -> 1.67 us  [body(): return result.reshape(LAGS, REACH, chans).transpose(1, 0, 2)[None]]
    ge x1 -> x0, other arithmetic: 0.66 us -> none  [body(): held = pair_owner[0] >= 0]
where the time goes in v7:
time: 49.9 us; the launch traced here: 49.7 us
  Pallas kernels  48 us (96%)
  local copies, waits for them, and re-layouts  1.67 us (3%)
    pallas_call x1, Pallas kernels, body(): pl.pallas_call(functools.partial(kernel, groups, planes), out_shape=jax.S...  48 us
    reshape x1, local copies, waits for them, and re-layouts, body(): return result.reshape(LAGS, REACH, chans).transpose(1, 0, 2)[None]  1.67 us

profile of v7, /device:TPU:0, one launch (start us, length us, event | category | flops | bytes accessed | tf_op | source)
XLA Modules:
  0.0 49.7 jit_solution(10850969807723496792)
XLA Ops:
  0.0 48.0 %correlate.1 = f32[404,128]{1,0:T(8,128)} custom-call(bf16[24,128,1024]{2,1,0:T(8,128)(2,1)} %bitcast.5, s32[24,1024]{1,0:T(8,128)} %bitcast.6, s32[1,4]{1,0:T(1,128)} %owners.1, bf16[1024,512]{1,0:T(8,128)(2,1)} %constant.6.clone.forward, bf16[512,256]{1,0:T(8,128)(2,1)} %constant.7.clone.smoother_hbm, bf16[2,768,128]{2,1,0:T(8,128)(2,1)} %constant.8.clone.inverse_hbm), custom_call_target="tpu_custom_call" | custom-call | tf_op jit(solution)/shard_map/correlate/pallas_call | solution.py:399
  48.1 1.7 %reshape.3 = f32[101,4,128]{2,1,0:T(4,128)} reshape(f32[404,128]{1,0:T(8,128)} %correlate.1) | data formatting | bytes 413696 | tf_op jit(solution)/shard_map/reshape | solution.py:438

commit v8 on v7

--- a/solution.py
+++ b/solution.py
@@ -87,7 +87,7 @@
     small_base = 4 * z - 4 + 6 * y
 
     def channel_start(p):
-        return (p % 2) * 64 + ((p // 2) % 2) * 32 + (p // 4) * 16
+        return (p % 2) * 64 + lax.rem(p // 2 + core, 2) * 32 + (p // 4) * 16
 
     def load(p):
         return pltpu.make_async_copy(
@@ -186,7 +186,7 @@
 
     def produce(p, carry):
         e = lax.rem(p, 2)
-        c = lax.rem(p // 2, 2)
+        c = lax.rem(p // 2 + core, 2)
         half = p // 4
         load(p).wait()
 
@@ -325,7 +325,7 @@
         def _():
             for c in range(2):
                 for e in range(2):
-                    chunk_copies(e, c, q + AHEAD, start, True)
+                    chunk_copies(e, lax.rem(c + core, 2), q + AHEAD, start, True)
 
         cross(big, q, BIG, 0)
 

time: 49.9 us -> 50.3 us (level)
  no operation moved by 1% of the time
where the time goes in v8:
time: 50.3 us; the launch traced here: 50.1 us
  Pallas kernels  48.5 us (96%)
  local copies, waits for them, and re-layouts  1.67 us (3%)
    pallas_call x1, Pallas kernels, body(): pl.pallas_call(functools.partial(kernel, groups, planes), out_shape=jax.S...  48.5 us
    reshape x1, local copies, waits for them, and re-layouts, body(): return result.reshape(LAGS, REACH, chans).transpose(1, 0, 2)[None]  1.67 us

profile of v8, /device:TPU:0, one launch (start us, length us, event | category | flops | bytes accessed | tf_op | source)
XLA Modules:
  0.0 50.1 jit_solution(11522721796972547090)
XLA Ops:
  0.0 48.5 %correlate.1 = f32[404,128]{1,0:T(8,128)} custom-call(bf16[24,128,1024]{2,1,0:T(8,128)(2,1)} %bitcast.5, s32[24,1024]{1,0:T(8,128)} %bitcast.6, s32[1,4]{1,0:T(1,128)} %owners.1, bf16[1024,512]{1,0:T(8,128)(2,1)} %constant.6.clone.forward, bf16[512,256]{1,0:T(8,128)(2,1)} %constant.7.clone.smoother_hbm, bf16[2,768,128]{2,1,0:T(8,128)(2,1)} %constant.8.clone.inverse_hbm), custom_call_target="tpu_custom_call" | custom-call | tf_op jit(solution)/shard_map/correlate/pallas_call | solution.py:399
  48.5 1.7 %reshape.3 = f32[101,4,128]{2,1,0:T(4,128)} reshape(f32[404,128]{1,0:T(8,128)} %correlate.1) | data formatting | bytes 413696 | tf_op jit(solution)/shard_map/reshape | solution.py:438
